TPU v7x, 256 devices: a whole 4x4x8 slice. The times are simulated.
256 devices in a mesh: section: 4 (over y), expert: 64 (over z, x, core).
Axes of the slice: x: 4, y: 4, z: 8, core: 2. Of those that a mesh axis runs over, the one named last changes fastest.
Arguments:
- inputs: bfloat16 [1, 2048, 2048], P(None, 'expert'), may hold values from -6 to 6
- norm_gain: float32 [4, 2048], P('section'), may hold values from 0.25 to 1.75
- expert_ids: int32 [4, 1, 2048, 2], P('section', None, 'expert'), may hold values from 0 to 63, all different within a row; in each aligned block of 32 rows (0 to 31, 32 to 63, ..., all dimensions but the last counted through in order) at most 2 rows name the same one
- route_weights: float32 [4, 1, 2048, 2], P('section', None, 'expert'), may hold values from 0.3 to 1
- gate_codes: bfloat16 [4, 64, 2048, 768], P('section', 'expert'), may hold values from 0 to 3, as said below
- up_codes: bfloat16 [4, 64, 2048, 768], P('section', 'expert'), may hold values from 0 to 3, as said below
- down_codes: bfloat16 [4, 64, 768, 2048], P('section', 'expert'), may hold values from 0 to 3, as said below
- gate_steps: float32 [4, 64, 32, 768], P('section', 'expert'), may hold values from 0.5 to 2
- up_steps: float32 [4, 64, 32, 768], P('section', 'expert'), may hold values from 0.5 to 2
- down_steps: float32 [4, 64, 12, 2048], P('section', 'expert'), may hold values from 0.5 to 2
- out_grad: bfloat16 [1, 2048, 2048], P(None, 'expert'), may hold values from -6 to 6
Outputs:
- layer_outputs: bfloat16 [4, 1, 2048, 2048], P('section', None, 'expert')
- input_grads: bfloat16 [4, 1, 2048, 2048], P('section', None, 'expert')
- gate_step_grads: float32 [4, 64, 32, 768], P('section', 'expert')
- up_step_grads: float32 [4, 64, 32, 768], P('section', 'expert')
- down_step_grads: float32 [4, 64, 12, 2048], P('section', 'expert')
Inputs may be any that keep to these rules, and one draw needn't show every extreme that they name: `expert_ids`: each token names 2 different experts. Within one layer and one micro-batch, at most 2 of the 32 tokens of one device (aligned blocks of 32 tokens) name any one expert; the bound is reached in some of these blocks. `gate_codes`: integer codes. `up_codes`: integer codes. `down_codes`: integer codes.
All inputs are finite; a program needn't handle non-finite values.
Results may differ from a plain program's by a relative error of at most 0.028.
Values may be sent and summed in bfloat16 or wider, within the bound.
A program may use at most 128 MiB of HBM per device.

v0:
```python
import functools

import jax
import jax.numpy as jnp
from jax import lax
from jax.experimental import pallas as pl
from jax.experimental.pallas import tpu as pltpu
from jax.sharding import PartitionSpec as P

MESH = pl.DeviceIdType.MESH
BF16 = jnp.bfloat16
F32 = jnp.float32

SECTIONS, NZ, NX, NC = 4, 8, 4, 2
EXPERTS = NZ * NX * NC
TOKENS, TOP, SLOTS = 32, 2, 2
WIDTH, HIDDEN, GROUP = 2048, 768, 64
PIECES, LANES = 8, 256
TILE = SLOTS * PIECES
CHAINS = 2
SOURCES = EXPERTS // CHAINS
ROWS = SOURCES * SLOTS

NT = (((1,), (1,)), ((), ()))
TN = (((0,), (0,)), ((), ()))


def dot(a, b, dims=(((1,), (0,)), ((), ()))):
    return lax.dot_general(a, b, dims, preferred_element_type=F32)


def iota(shape, dim):
    return lax.broadcasted_iota(jnp.int32, shape, dim)


def route_info(ids, weights):
    lane = iota((TOKENS, 128), 1)
    first, second = ids[:, 0:1], ids[:, 1:2]
    hot0 = (lane == first).astype(F32)
    hot1 = (lane == second).astype(F32)
    earlier = (iota((TOKENS, TOKENS), 1) < iota((TOKENS, TOKENS), 0)).astype(BF16)
    count = dot(earlier, (hot0 + hot1).astype(BF16))
    slot0 = first.astype(F32) * SLOTS + jnp.sum(hot0 * count, axis=1, keepdims=True)
    slot1 = second.astype(F32) * SLOTS + jnp.sum(hot1 * count, axis=1, keepdims=True)
    info = jnp.where(lane == 0, slot0, 0.0) + jnp.where(lane == 1, slot1, 0.0)
    info = info + jnp.where(lane == 2, weights[:, 0:1], 0.0)
    return info + jnp.where(lane == 3, weights[:, 1:2], 0.0)


def place_matrix(info, weighted):
    spread = (iota((TOKENS, TOKENS * PIECES), 1) // PIECES == iota((TOKENS, TOKENS * PIECES), 0)).astype(BF16)
    cols = dot(info.astype(BF16), spread, TN)
    shape = (EXPERTS * TILE, TOKENS * PIECES)
    piece = iota((1, TOKENS * PIECES), 1) % PIECES
    at0 = cols[0:1, :].astype(jnp.int32) * PIECES + piece
    at1 = cols[1:2, :].astype(jnp.int32) * PIECES + piece
    row = iota(shape, 0)
    w0, w1 = (cols[2:3, :], cols[3:4, :]) if weighted else (1.0, 1.0)
    return (jnp.where(row == at0, w0, 0.0) + jnp.where(row == at1, w1, 0.0)).astype(BF16)


def take_matrix(info, weighted):
    spread = (iota((TOKENS * PIECES, TOKENS), 0) // PIECES == iota((TOKENS * PIECES, TOKENS), 1)).astype(BF16)
    rows = dot(spread, info.astype(BF16))
    shape = (TOKENS * PIECES, EXPERTS * TILE)
    piece = iota((TOKENS * PIECES, 1), 0) % PIECES
    at0 = rows[:, 0:1].astype(jnp.int32) * PIECES + piece
    at1 = rows[:, 1:2].astype(jnp.int32) * PIECES + piece
    col = iota(shape, 1)
    w0, w1 = (rows[:, 2:3], rows[:, 3:4]) if weighted else (1.0, 1.0)
    return (jnp.where(col == at0, w0, 0.0) + jnp.where(col == at1, w1, 0.0)).astype(BF16)


def token_sum(values):
    shaped = values.reshape(TOKENS, PIECES, LANES)
    total = jnp.sum(jnp.sum(shaped, axis=2, keepdims=True), axis=1, keepdims=True)
    return jnp.broadcast_to(total, (TOKENS, PIECES, LANES)).reshape(TOKENS * PIECES, LANES)


def kernel(
    x_ref, gain_ref, ids_ref, wts_ref, gc_hbm, uc_hbm, dc_hbm, gs_ref, us_ref, ds_ref, og_ref,
    lo_ref, ig_ref, gg_ref, ug_ref, dg_ref,
    gcode, ucode, dcode, w_gu, w_d,
    f_recv, r_recv, b_recv, q_recv, send_f, send_b, r_send, q_send,
    place_a, place_b, take_w, take_1,
    h_in, h_out, g_in, g_out, info_own, info_next, info_prev, gain8,
    wide, home, x_rows, pre, act, cot, gu_cot,
    code_sem, f_sem, r_sem, b_sem, q_sem, far_sem, sent_f, sent_b, sent_r, sent_q, sent_far,
):
    s = lax.axis_index("section")
    e = lax.axis_index("expert")
    z, x, c = e // (NX * NC), (e // NC) % NX, e % NC
    first, last = s == 0, s == SECTIONS - 1

    def index_of(zz, xx, cc):
        return (zz * NX + xx) * NC + cc

    barrier = pltpu.get_barrier_semaphore()

    def greet(section):
        def one(k, carry):
            pl.semaphore_signal(barrier, inc=1, device_id=(section, lax.rem(e + k, EXPERTS)), device_id_type=MESH)
            return carry
        return one

    lax.fori_loop(1, EXPERTS, greet(s), 0)

    @pl.when(s > 0)
    def _():
        lax.fori_loop(0, EXPERTS, greet(s - 1), 0)

    @pl.when(s < SECTIONS - 1)
    def _():
        lax.fori_loop(0, EXPERTS, greet(s + 1), 0)

    loads = [
        pltpu.make_async_copy(gc_hbm, gcode, code_sem.at[0]),
        pltpu.make_async_copy(uc_hbm, ucode, code_sem.at[1]),
        pltpu.make_async_copy(dc_hbm, dcode, code_sem.at[2]),
    ]
    for load in loads:
        load.start()

    info_own[...] = route_info(ids_ref[...], wts_ref[...])
    for p in range(PIECES):
        gain8[p : p + 1, :] = gain_ref[0:1, p * LANES : (p + 1) * LANES]

    def to_pieces(source):
        for p in range(PIECES):
            part = source[:, p * LANES : (p + 1) * LANES].astype(F32)
            for half in range(2):
                home[half, pl.ds(p, TOKENS, stride=PIECES), :] = part[:, half * 128 : (half + 1) * 128]
        return jnp.concatenate([home[0], home[1]], axis=1)

    def from_pieces(values, out_ref):
        for half in range(2):
            home[half] = values[:, half * 128 : (half + 1) * 128]
        for p in range(PIECES):
            for half in range(2):
                lanes = pl.ds(p * LANES + half * 128, 128)
                out_ref[:, lanes] = home[half, pl.ds(p, TOKENS, stride=PIECES), :].astype(out_ref.dtype)

    def far_z(j):
        return lax.rem(z + jnp.where(j % 2 == 0, 4 + j // 2, 3 - j // 2), NZ)

    X_ORDER = (2, 1, 3, 0)

    def remote(src, dst, ssem, rsem, section, target):
        pltpu.make_async_remote_copy(
            src_ref=src, dst_ref=dst, send_sem=ssem, recv_sem=rsem, device_id=(section, target), device_id_type=MESH
        ).start()

    chain, order = c, z * NX + x

    def scatter(place, values, buffer, recv, rsem, ssem, section, own_plane):
        def plane(j, skip):
            zz = far_z(j)
            block = pl.ds(pl.multiple_of(zz * NX * NC * TILE, 128), NX * NC * TILE)
            packed = dot(place[block, :], values).astype(BF16)
            buffer[pl.ds(zz * NX * NC, NX * NC)] = packed.reshape(NX * NC, TILE, LANES)
            for dx in X_ORDER:
                for dc in (1, 0):
                    target = index_of(zz, lax.rem(x + dx, NX), lax.rem(c + dc, NC))
                    if skip and dx == 0 and dc == 0:
                        pltpu.make_async_copy(buffer.at[e], recv.at[chain, order], rsem.at[chain]).start()
                    else:
                        remote(buffer.at[target], recv.at[chain, order], ssem, rsem.at[chain], section, target)

        def loop(j, carry):
            plane(j, False)
            return carry

        lax.fori_loop(0, NZ - 1, loop, 0)
        plane(NZ - 1, own_plane)

    def give_back(ch, buffer, recv, rsem, ssem):
        def plane(j, own):
            zz = far_z(j)
            block = pl.ds(pl.multiple_of(zz * NX * TILE, 64), NX * TILE)
            rows = jnp.concatenate([wide[0, block, :], wide[1, block, :]], axis=1).astype(BF16)
            buffer[ch, pl.ds(zz * NX, NX)] = rows.reshape(NX, TILE, LANES)
            for dx in X_ORDER:
                xx = lax.rem(x + dx, NX)
                target = index_of(zz, xx, ch)
                src, dst = buffer.at[ch, zz * NX + xx], recv.at[e]
                if own and dx == 0:
                    @pl.when(ch == c)
                    def _():
                        pltpu.make_async_copy(src, dst, rsem).start()

                    @pl.when(ch != c)
                    def _():
                        remote(src, dst, ssem, rsem, s, target)
                else:
                    remote(src, dst, ssem, rsem, s, target)

        def loop(j, carry):
            plane(j, False)
            return carry

        lax.fori_loop(0, NZ - 1, loop, 0)
        plane(NZ - 1, True)

    def wait_all(ref, sem):
        pltpu.make_async_copy(ref, ref, sem).wait()

    own_info = info_own[...]

    @pl.when(first)
    def _():
        values = to_pieces(x_ref)
        h_in[...] = values.astype(BF16)
        place_b[...] = place_matrix(own_info, False)

    @pl.when(last)
    def _():
        values = to_pieces(og_ref)
        g_in[...] = values.astype(BF16)
        place_a[...] = place_matrix(own_info, True)

    neighbours = jnp.where(first, 0, 1) + jnp.where(last, 0, 1)
    pl.semaphore_wait(barrier, EXPERTS - 1 + neighbours * EXPERTS)

    @pl.when(first)
    def _():
        scatter(place_b, h_in[...], send_b, f_recv, f_sem, sent_b, 0, True)

    @pl.when(last)
    def _():
        scatter(place_a, g_in[...], send_f, b_recv, b_sem, sent_f, SECTIONS - 1, True)

    @pl.when(s > 0)
    def _():
        remote(info_own, info_next, sent_far.at[0], far_sem.at[0], s - 1, e)

    @pl.when(s < SECTIONS - 1)
    def _():
        remote(info_own, info_prev, sent_far.at[1], far_sem.at[1], s + 1, e)

    def dequant(code, steps, out, col, fan_in, groups):
        def one(g, carry):
            rows = pl.ds(pl.multiple_of(g * GROUP, GROUP), GROUP)
            scale = steps[pl.ds(g, 1), :] * fan_in ** (-0.5)
            width = code.shape[1]
            out[rows, col : col + width] = ((code[rows, :].astype(F32) - 1.5) * scale).astype(BF16)
            return carry
        lax.fori_loop(0, groups, one, 0)

    loads[0].wait()
    dequant(gcode, gs_ref, w_gu, 0, WIDTH, WIDTH // GROUP)
    loads[1].wait()
    dequant(ucode, us_ref, w_gu, HIDDEN, WIDTH, WIDTH // GROUP)
    loads[2].wait()
    dequant(dcode, ds_ref, w_d, 0, HIDDEN, HIDDEN // GROUP)

    take_w[...] = take_matrix(own_info, True)
    take_1[...] = take_matrix(own_info, False)

    @pl.when(s < SECTIONS - 1)
    def _():
        wait_all(info_next, far_sem.at[0])
        place_a[...] = place_matrix(info_next[...], False)

    @pl.when(s > 0)
    def _():
        wait_all(info_prev, far_sem.at[1])
        place_b[...] = place_matrix(info_prev[...], True)

    def spread_out(recv, ch):
        flat = recv[ch].reshape(SOURCES * TILE, LANES).astype(F32)
        for half in range(2):
            wide[half] = flat[:, half * 128 : (half + 1) * 128]
        return [
            jnp.concatenate([wide[half, pl.ds(p, ROWS, stride=PIECES), :] for half in range(2)], axis=1)
            for p in range(PIECES)
        ]

    def collect(p, part):
        for half in range(2):
            wide[half, pl.ds(p, ROWS, stride=PIECES), :] = part[:, half * 128 : (half + 1) * 128]

    def rows_of(ch):
        return pl.ds(pl.multiple_of(ch * ROWS, ROWS), ROWS)

    def gates(ch):
        wait_all(f_recv.at[ch], f_sem.at[ch])
        parts = spread_out(f_recv, ch)
        square = functools.reduce(lambda a, b: a + b, [jnp.sum(q * q, axis=1, keepdims=True) for q in parts])
        inv = lax.rsqrt(square * (1.0 / WIDTH) + 1e-06)
        rows = rows_of(ch)
        for p in range(PIECES):
            lanes = slice(p * LANES, (p + 1) * LANES)
            x_rows[rows, lanes] = (parts[p] * inv * gain_ref[0:1, lanes]).astype(BF16)
        pre[rows, :] = dot(x_rows[rows, :], w_gu[...])
        gate, up = pre[rows, :HIDDEN], pre[rows, HIDDEN:]
        act[rows, :] = (gate * jax.nn.sigmoid(gate) * up).astype(BF16)

    def down(ch):
        rows = rows_of(ch)
        for p in range(PIECES):
            collect(p, dot(act[rows, :], w_d[:, p * LANES : (p + 1) * LANES]))
        give_back(ch, r_send, r_recv, r_sem, sent_r)

    def backward(ch):
        wait_all(b_recv.at[ch], b_sem.at[ch])
        parts = spread_out(b_recv, ch)
        rows = rows_of(ch)
        for p in range(PIECES):
            cot[rows, p * LANES : (p + 1) * LANES] = parts[p].astype(BF16)
        act_cot = dot(cot[rows, :], w_d[...], NT)
        gate, up = pre[rows, :HIDDEN], pre[rows, HIDDEN:]
        sig = jax.nn.sigmoid(gate)
        gu_cot[rows, :HIDDEN] = (act_cot * up * sig * (1.0 + gate * (1.0 - sig))).astype(BF16)
        gu_cot[rows, HIDDEN:] = (act_cot * gate * sig).astype(BF16)
        for p in range(PIECES):
            collect(p, dot(gu_cot[rows, :], w_gu[p * LANES : (p + 1) * LANES, :], NT))
        give_back(ch, q_send, q_recv, q_sem, sent_q)

    def each_chain(step):
        def one(ch, carry):
            step(ch)
            return carry
        lax.fori_loop(0, CHAINS, one, 0)

    def home_forward():
        wait_all(r_recv, r_sem)
        mixed = dot(take_w[...], r_recv[...].reshape(EXPERTS * TILE, LANES))

        @pl.when(s > 0)
        def _():
            wait_all(h_in, far_sem.at[2])

        return (h_in[...].astype(F32) + mixed).astype(BF16)

    def home_backward():
        wait_all(q_recv, q_sem)
        normed_cot = dot(take_1[...], q_recv[...].reshape(EXPERTS * TILE, LANES))

        @pl.when(s < SECTIONS - 1)
        def _():
            wait_all(g_in, far_sem.at[3])

        hidden = h_in[...].astype(F32)
        inv = lax.rsqrt(token_sum(hidden * hidden) * (1.0 / WIDTH) + 1e-06)
        gain = jnp.broadcast_to(gain8[...].reshape(1, PIECES, LANES), (TOKENS, PIECES, LANES))
        scaled = gain.reshape(TOKENS * PIECES, LANES) * normed_cot
        mean = token_sum(scaled * hidden) * (1.0 / WIDTH)
        total = g_in[...].astype(F32) + inv * scaled - hidden * (inv * inv * inv) * mean
        return total.astype(BF16)

    def step_grads():
        def gate_up(i, carry):
            rows = pl.ds(pl.multiple_of(i * 256, 256), 256)
            for code, out, col in ((gcode, gg_ref, 0), (ucode, ug_ref, HIDDEN)):
                grad = dot(x_rows[:, rows], gu_cot[:, col : col + HIDDEN], TN)
                grad = grad * (code[rows, :].astype(F32) - 1.5)
                summed = jnp.sum(grad.reshape(256 // GROUP, GROUP, HIDDEN), axis=1) * WIDTH ** (-0.5)
                for g in range(256 // GROUP):
                    out[pl.ds(i * (256 // GROUP) + g, 1), :] = summed[g : g + 1, :]
            return carry

        lax.fori_loop(0, WIDTH // 256, gate_up, 0)

        def down_part(i, carry):
            rows = pl.ds(pl.multiple_of(i * 256, 256), 256)
            for col in range(0, WIDTH, 1024):
                grad = dot(act[:, rows], cot[:, col : col + 1024], TN)
                grad = grad * (dcode[rows, col : col + 1024].astype(F32) - 1.5)
                summed = jnp.sum(grad.reshape(256 // GROUP, GROUP, 1024), axis=1) * HIDDEN ** (-0.5)
                for g in range(256 // GROUP):
                    dg_ref[pl.ds(i * (256 // GROUP) + g, 1), col : col + 1024] = summed[g : g + 1, :]
            return carry

        lax.fori_loop(0, HIDDEN // 256, down_part, 0)

    @pl.when(s < SECTIONS - 1)
    def _():
        def forward(ch):
            gates(ch)
            down(ch)

        each_chain(forward)
        h_out[...] = home_forward()
        scatter(place_a, h_out[...], send_f, f_recv, f_sem, sent_f, s + 1, False)
        remote(h_out, h_in, sent_far.at[2], far_sem.at[2], s + 1, e)
        from_pieces(h_out[...].astype(F32), lo_ref)
        each_chain(backward)

    @pl.when(last)
    def _():
        def turn(ch):
            gates(ch)
            backward(ch)

        each_chain(turn)
        each_chain(down)
        h_out[...] = home_forward()
        from_pieces(h_out[...].astype(F32), lo_ref)

    @pl.when(first)
    def _():
        step_grads()

    g_out[...] = home_backward()

    @pl.when(s > 0)
    def _():
        scatter(place_b, g_out[...], send_b, b_recv, b_sem, sent_b, s - 1, False)
        remote(g_out, g_in, sent_far.at[3], far_sem.at[3], s - 1, e)

    from_pieces(g_out[...].astype(F32), ig_ref)

    @pl.when(s > 0)
    def _():
        step_grads()

    @pl.when(first)
    def _():
        wait_all(send_f, sent_f)
        wait_all(send_b.at[pl.ds(0, EXPERTS - 1)], sent_b)

    @pl.when(last)
    def _():
        wait_all(send_f.at[pl.ds(0, EXPERTS - 1)], sent_f)
        wait_all(send_b, sent_b)

    @pl.when(jnp.logical_and(s > 0, s < SECTIONS - 1))
    def _():
        wait_all(send_f, sent_f)
        wait_all(send_b, sent_b)

    wait_all(send_f.at[pl.ds(0, EXPERTS - 1)], sent_r)
    wait_all(send_f.at[pl.ds(0, EXPERTS - 1)], sent_q)

    @pl.when(s > 0)
    def _():
        wait_all(info_own, sent_far.at[0])
        wait_all(g_out, sent_far.at[3])

    @pl.when(s < SECTIONS - 1)
    def _():
        wait_all(info_own, sent_far.at[1])
        wait_all(h_out, sent_far.at[2])


def body(inputs, norm_gain, expert_ids, route_weights, gate_codes, up_codes, down_codes, gate_steps, up_steps, down_steps, out_grad):
    vmem = pl.BlockSpec(memory_space=pltpu.VMEM)
    hbm = pl.BlockSpec(memory_space=pl.ANY)
    message = (TILE, LANES)
    pieces = (TOKENS * PIECES, LANES)
    slots = EXPERTS * TILE
    both = CHAINS * ROWS
    scratch = [
        pltpu.VMEM((WIDTH, HIDDEN), BF16),
        pltpu.VMEM((WIDTH, HIDDEN), BF16),
        pltpu.VMEM((HIDDEN, WIDTH), BF16),
        pltpu.VMEM((WIDTH, 2 * HIDDEN), BF16),
        pltpu.VMEM((HIDDEN, WIDTH), BF16),
        pltpu.VMEM((CHAINS, SOURCES) + message, BF16),
        pltpu.VMEM((EXPERTS,) + message, BF16),
        pltpu.VMEM((CHAINS, SOURCES) + message, BF16),
        pltpu.VMEM((EXPERTS,) + message, BF16),
        pltpu.VMEM((EXPERTS,) + message, BF16),
        pltpu.VMEM((EXPERTS,) + message, BF16),
        pltpu.VMEM((CHAINS, SOURCES) + message, BF16),
        pltpu.VMEM((CHAINS, SOURCES) + message, BF16),
        pltpu.VMEM((slots, TOKENS * PIECES), BF16),
        pltpu.VMEM((slots, TOKENS * PIECES), BF16),
        pltpu.VMEM((TOKENS * PIECES, slots), BF16),
        pltpu.VMEM((TOKENS * PIECES, slots), BF16),
        pltpu.VMEM(pieces, BF16),
        pltpu.VMEM(pieces, BF16),
        pltpu.VMEM(pieces, BF16),
        pltpu.VMEM(pieces, BF16),
        pltpu.VMEM((TOKENS, 128), F32),
        pltpu.VMEM((TOKENS, 128), F32),
        pltpu.VMEM((TOKENS, 128), F32),
        pltpu.VMEM((PIECES, LANES), F32),
        pltpu.VMEM((2, SOURCES * TILE, 128), F32),
        pltpu.VMEM((2, TOKENS * PIECES, 128), F32),
        pltpu.VMEM((both, WIDTH), BF16),
        pltpu.VMEM((both, 2 * HIDDEN), F32),
        pltpu.VMEM((both, HIDDEN), BF16),
        pltpu.VMEM((both, WIDTH), BF16),
        pltpu.VMEM((both, 2 * HIDDEN), BF16),
        pltpu.SemaphoreType.DMA((3,)),
        pltpu.SemaphoreType.DMA((CHAINS,)),
        pltpu.SemaphoreType.DMA,
        pltpu.SemaphoreType.DMA((CHAINS,)),
        pltpu.SemaphoreType.DMA,
        pltpu.SemaphoreType.DMA((4,)),
        pltpu.SemaphoreType.DMA,
        pltpu.SemaphoreType.DMA,
        pltpu.SemaphoreType.DMA,
        pltpu.SemaphoreType.DMA,
        pltpu.SemaphoreType.DMA((4,)),
    ]
    outs = pl.pallas_call(
        kernel,
        out_shape=(
            jax.ShapeDtypeStruct((TOKENS, WIDTH), BF16),
            jax.ShapeDtypeStruct((TOKENS, WIDTH), BF16),
            jax.ShapeDtypeStruct((WIDTH // GROUP, HIDDEN), F32),
            jax.ShapeDtypeStruct((WIDTH // GROUP, HIDDEN), F32),
            jax.ShapeDtypeStruct((HIDDEN // GROUP, WIDTH), F32),
        ),
        in_specs=[vmem] * 4 + [hbm] * 3 + [vmem] * 4,
        out_specs=[vmem] * 5,
        scratch_shapes=scratch,
        compiler_params=pltpu.CompilerParams(
            collective_id=0, has_side_effects=True, vmem_limit_bytes=48 * 1024 * 1024
        ),
    )(
        inputs[0], norm_gain, expert_ids[0, 0], route_weights[0, 0],
        gate_codes[0, 0], up_codes[0, 0], down_codes[0, 0],
        gate_steps[0, 0], up_steps[0, 0], down_steps[0, 0], out_grad[0],
    )
    layer_out, input_grad, gate_grad, up_grad, down_grad = outs
    return (layer_out[None, None], input_grad[None, None], gate_grad[None, None], up_grad[None, None], down_grad[None, None])


def solution(mesh):
    in_specs = (
        P(None, "expert", None),
        P("section", None),
        P("section", None, "expert", None),
        P("section", None, "expert", None),
        P("section", "expert", None, None),
        P("section", "expert", None, None),
        P("section", "expert", None, None),
        P("section", "expert", None, None),
        P("section", "expert", None, None),
        P("section", "expert", None, None),
        P(None, "expert", None),
    )
    out_specs = (
        P("section", None, "expert", None),
        P("section", None, "expert", None),
        P("section", "expert", None, None),
        P("section", "expert", None, None),
        P("section", "expert", None, None),
    )
    return jax.shard_map(body, mesh=mesh, in_specs=in_specs, out_specs=out_specs, check_vma=False)
```

profile of v0, /device:TPU:1, one launch (start us, length us, event | category | flops | bytes accessed | tf_op | source)
XLA Modules:
  0.0 239.6 jit_solution(882594414689354068)
XLA Ops:
  0.6 0.8 copy.16.ids_ref
  1.4 0.8 copy.17.wts_ref
  2.2 0.9 copy.21
  3.1 0.0 copy-start
  3.1 1.9 copy-done
  5.0 0.0 copy-start.1
  5.0 0.9 copy-done.1
  5.9 0.0 copy-start.2
  5.9 0.9 copy-done.2
  6.8 0.0 copy-start.3
  6.8 0.9 copy-done.3
  7.7 0.0 copy-start.4
  7.7 0.9 copy-done.4
  8.6 0.0 copy-start.5
  8.6 0.7 copy-done.5
  9.3 226.9 %shard_map.146 = (bf16[32,2048]{1,0:T(8,128)(2,1)S(1)}, bf16[32,2048]{1,0:T(8,128)(2,1)S(1)}, f32[32,768]{1,0:T(8,128)S(1)}, f32[32,768]{1,0:T(8,128)S(1)}, f32[12,2048]{1,0:T(8,128)S(1)}) custom-call(bf16[32,2048]{1,0:T(8,128)(2,1)S(1)} %bitcast.19, f32[1,2048]{1,0:T(1,128)S(1)} %copy-done.5, s32[32,2]{1,0:T(8,128)S(1)} %copy.16.ids_ref, ...), custom_call_target="tpu_custom_call" | custom-call | tf_op jit(solution)/shard_map/pallas_call | solution.py:498
  236.2 0.7 copy.18
  237.0 0.7 copy.26
  237.6 0.7 copy.27
  238.3 0.6 copy.28
  238.9 0.6 copy.29
Async XLA Ops:
  3.1 1.9 copy-start
  5.0 0.9 copy-start.1
  5.9 0.9 copy-start.2
  6.8 0.9 copy-start.3
  7.7 0.9 copy-start.4
  8.6 0.7 copy-start.5
where the time goes:
time: 240 us
  Pallas kernels  227 us (95%)
  local copies, waits for them, and re-layouts  11.9 us (5%)
    pallas_call x1, Pallas kernels, body(): pl.pallas_call(kernel, out_shape=(jax.ShapeDtypeStruct((TOKENS, WIDTH), B...  227 us
    unnamed x18, local copies, waits for them, and re-layouts  10.4 us

commit v1 on v0

v1 whole, which is shorter than its diff:
```python
import functools

import jax
import jax.numpy as jnp
from jax import lax
from jax.experimental import pallas as pl
from jax.experimental.pallas import tpu as pltpu
from jax.sharding import PartitionSpec as P

MESH = pl.DeviceIdType.MESH
BF16 = jnp.bfloat16
F32 = jnp.float32

SECTIONS, NZ, NX, NC = 4, 8, 4, 2
EXPERTS = NZ * NX * NC
TOKENS, TOP, SLOTS = 32, 2, 2
WIDTH, HIDDEN, GROUP = 2048, 768, 64
PIECES, LANES = 8, 256
TILE = SLOTS * PIECES
CHAINS = 2
SOURCES = EXPERTS // CHAINS
ROWS = SOURCES * SLOTS

NT = (((1,), (1,)), ((), ()))
TN = (((0,), (0,)), ((), ()))


def dot(a, b, dims=(((1,), (0,)), ((), ()))):
    return lax.dot_general(a, b, dims, preferred_element_type=F32)


def iota(shape, dim):
    return lax.broadcasted_iota(jnp.int32, shape, dim)


def route_info(ids, weights):
    lane = iota((TOKENS, 128), 1)
    same = iota((TOKENS, TOKENS), 0) == iota((TOKENS, TOKENS), 1)
    first, second = [jnp.sum(jnp.where(same, ids[k : k + 1, :], 0), axis=1, keepdims=True) for k in range(TOP)]
    weight0, weight1 = [jnp.sum(jnp.where(same, weights[k : k + 1, :], 0.0), axis=1, keepdims=True) for k in range(TOP)]
    hot0 = (lane == first).astype(F32)
    hot1 = (lane == second).astype(F32)
    earlier = (iota((TOKENS, TOKENS), 1) < iota((TOKENS, TOKENS), 0)).astype(BF16)
    count = dot(earlier, (hot0 + hot1).astype(BF16))
    slot0 = first.astype(F32) * SLOTS + jnp.sum(hot0 * count, axis=1, keepdims=True)
    slot1 = second.astype(F32) * SLOTS + jnp.sum(hot1 * count, axis=1, keepdims=True)
    info = jnp.where(lane == 0, slot0, 0.0) + jnp.where(lane == 1, slot1, 0.0)
    info = info + jnp.where(lane == 2, weight0, 0.0)
    return info + jnp.where(lane == 3, weight1, 0.0)


def place_matrix(info, weighted):
    spread = (iota((TOKENS, TOKENS * PIECES), 1) // PIECES == iota((TOKENS, TOKENS * PIECES), 0)).astype(BF16)
    cols = dot(info.astype(BF16), spread, TN)
    shape = (EXPERTS * TILE, TOKENS * PIECES)
    piece = iota((1, TOKENS * PIECES), 1) % PIECES
    at0 = cols[0:1, :].astype(jnp.int32) * PIECES + piece
    at1 = cols[1:2, :].astype(jnp.int32) * PIECES + piece
    row = iota(shape, 0)
    w0, w1 = (cols[2:3, :], cols[3:4, :]) if weighted else (1.0, 1.0)
    return (jnp.where(row == at0, w0, 0.0) + jnp.where(row == at1, w1, 0.0)).astype(BF16)


def take_matrix(info, weighted):
    spread = (iota((TOKENS * PIECES, TOKENS), 0) // PIECES == iota((TOKENS * PIECES, TOKENS), 1)).astype(BF16)
    rows = dot(spread, info.astype(BF16))
    shape = (TOKENS * PIECES, EXPERTS * TILE)
    piece = iota((TOKENS * PIECES, 1), 0) % PIECES
    at0 = rows[:, 0:1].astype(jnp.int32) * PIECES + piece
    at1 = rows[:, 1:2].astype(jnp.int32) * PIECES + piece
    col = iota(shape, 1)
    w0, w1 = (rows[:, 2:3], rows[:, 3:4]) if weighted else (1.0, 1.0)
    return (jnp.where(col == at0, w0, 0.0) + jnp.where(col == at1, w1, 0.0)).astype(BF16)


def token_sum(values):
    shaped = values.reshape(TOKENS, PIECES, LANES)
    total = jnp.sum(jnp.sum(shaped, axis=2, keepdims=True), axis=1, keepdims=True)
    return jnp.broadcast_to(total, (TOKENS, PIECES, LANES)).reshape(TOKENS * PIECES, LANES)


def home_plane(z, x):
    return lax.rem(z + x, SECTIONS)


def kernel(
    x_hbm, gain_hbm, ids_hbm, wts_hbm, gc_hbm, uc_hbm, dc_hbm, gs_hbm, us_hbm, ds_hbm, og_hbm,
    lo_ref, ig_ref, gg_ref, ug_ref, dg_ref,
    x_ref, og_ref, gain_ref, ids_ref, wts_ref, gs_ref, us_ref, ds_ref,
    gcode, ucode, dcode, w_gu, w_d,
    f_recv, r_recv, b_recv, q_recv, send_first, send_home, r_send, q_send,
    place_first, place_f, place_b, take_w, take_1, take_last,
    h_all, g_all, g_final, lo_buf, ig_buf, g1_buf, note_own, notes,
    wide, home, x_rows, pre, act, cot, gu_cot,
    load_sem, f_sem, r_sem, b_sem, q_sem, note_sem, lo_sem, ig_sem, g1_sem,
    sent_first, sent_home, sent_r, sent_q, sent_note, sent_lo, sent_ig, sent_g1, planes_sem,
):
    s = lax.axis_index("section")
    e = lax.axis_index("expert")
    z, x, c = e // (NX * NC), (e // NC) % NX, e % NC
    first, last = s == 0, s == SECTIONS - 1
    at_home = s == home_plane(z, x)

    def index_of(zz, xx, cc):
        return (zz * NX + xx) * NC + cc

    barrier = pltpu.get_barrier_semaphore()

    def greet(k, carry):
        pl.semaphore_signal(barrier, inc=1, device_id=(s, lax.rem(e + k, EXPERTS)), device_id_type=MESH)
        return carry

    lax.fori_loop(1, EXPERTS, greet, 0)
    for k in range(1, SECTIONS):
        pl.semaphore_signal(barrier, inc=1, device_id=(lax.rem(s + k, SECTIONS), e), device_id_type=MESH)

    pairs = [
        (ids_hbm, ids_ref), (wts_hbm, wts_ref), (x_hbm, x_ref), (gain_hbm, gain_ref), (og_hbm, og_ref),
        (gs_hbm, gs_ref), (gc_hbm, gcode), (us_hbm, us_ref), (uc_hbm, ucode), (ds_hbm, ds_ref), (dc_hbm, dcode),
    ]
    loads = [pltpu.make_async_copy(src, dst, load_sem.at[k]) for k, (src, dst) in enumerate(pairs)]
    for load in loads:
        load.start()

    def to_pieces(source):
        for p in range(PIECES):
            part = source[:, p * LANES : (p + 1) * LANES].astype(F32)
            for half in range(2):
                home[half, pl.ds(p, TOKENS, stride=PIECES), :] = part[:, half * 128 : (half + 1) * 128]
        return jnp.concatenate([home[0], home[1]], axis=1)

    def from_pieces(values, out_ref):
        for half in range(2):
            home[half] = values[:, half * 128 : (half + 1) * 128]
        for p in range(PIECES):
            for half in range(2):
                lanes = pl.ds(p * LANES + half * 128, 128)
                out_ref[:, lanes] = home[half, pl.ds(p, TOKENS, stride=PIECES), :].astype(out_ref.dtype)

    def far_z(j):
        return lax.rem(z + jnp.where(j % 2 == 0, 4 + j // 2, 3 - j // 2), NZ)

    def remote(src, dst, ssem, rsem, section, target):
        pltpu.make_async_remote_copy(
            src_ref=src, dst_ref=dst, send_sem=ssem, recv_sem=rsem, device_id=(section, target), device_id_type=MESH
        ).start()

    def send_or_copy(src, dst, ssem, rsem, section, target, own):
        @pl.when(own)
        def _():
            pltpu.make_async_copy(src, dst, rsem).start()

        @pl.when(jnp.logical_not(own))
        def _():
            remote(src, dst, ssem, rsem, section, target)

    def wait_all(ref, sem):
        pltpu.make_async_copy(ref, ref, sem).wait()

    chain, order = c, z * NX + x

    def scatter(place, values, buffer, recv, rsem, ssem, section):
        def pack(j):
            zz = far_z(j)
            block = pl.ds(pl.multiple_of(zz * NX * NC * TILE, 128), NX * NC * TILE)
            packed = dot(place[block, :], values).astype(BF16)
            buffer[pl.ds(zz * NX * NC, NX * NC)] = packed.reshape(NX * NC, TILE, LANES)

        def send(j, dx, dc):
            target = index_of(far_z(j), lax.rem(x + dx, NX), lax.rem(c + dc, NC))
            remote(buffer.at[target], recv.at[chain, order], ssem, rsem.at[chain], section, target)

        def farthest(j, carry):
            pack(j)
            send(j, 2, 1)
            send(j, 2, 0)
            return carry

        def middle(j, carry):
            for dx in (1, 3):
                send(j, dx, 1)
                send(j, dx, 0)
            return carry

        def line(j, carry):
            send(j, 0, 1)
            send(j, 0, 0)
            return carry

        lax.fori_loop(0, NZ, farthest, 0)
        lax.fori_loop(0, NZ, middle, 0)
        lax.fori_loop(0, NZ - 1, line, 0)
        send(NZ - 1, 0, 1)
        send_or_copy(buffer.at[e], recv.at[chain, order], ssem, rsem.at[chain], section, e, section == s)

    def give_back(ch, buffer, recv, rsem, ssem, in_plane):
        def unpack(j):
            zz = far_z(j)
            block = pl.ds(pl.multiple_of(zz * NX * TILE, 64), NX * TILE)
            rows = jnp.concatenate([wide[0, block, :], wide[1, block, :]], axis=1).astype(BF16)
            buffer[ch, pl.ds(zz * NX, NX)] = rows.reshape(NX, TILE, LANES)

        def place_of(j, dx):
            zz, xx = far_z(j), lax.rem(x + dx, NX)
            section = jnp.where(in_plane, s, home_plane(zz, xx))
            return buffer.at[ch, zz * NX + xx], section, index_of(zz, xx, ch)

        def send(j, dx):
            src, section, target = place_of(j, dx)
            remote(src, recv.at[e], ssem, rsem, section, target)

        def farthest(j, carry):
            unpack(j)
            send(j, 2)
            return carry

        def middle(j, carry):
            send(j, 1)
            send(j, 3)
            return carry

        def line(j, carry):
            send(j, 0)
            return carry

        lax.fori_loop(0, NZ, farthest, 0)
        lax.fori_loop(0, NZ, middle, 0)
        lax.fori_loop(0, NZ - 1, line, 0)
        src, section, target = place_of(NZ - 1, 0)
        send_or_copy(src, recv.at[e], ssem, rsem, section, target, jnp.logical_and(section == s, ch == c))

    loads[0].wait()
    loads[1].wait()
    loads[2].wait()
    loads[3].wait()
    loads[4].wait()
    note_own[0:TOKENS, 0:128] = route_info(ids_ref[...], wts_ref[...])
    note_own[0:TOKENS, 128:] = jnp.zeros((TOKENS, LANES - 128), F32)
    for p in range(PIECES):
        note_own[TOKENS + p : TOKENS + p + 1, :] = gain_ref[0:1, p * LANES : (p + 1) * LANES]
    own_info = note_own[0:TOKENS, 0:128]

    h_all[0] = to_pieces(x_ref).astype(BF16)

    @pl.when(first)
    def _():
        place_first[...] = place_matrix(own_info, False)

    g_all[SECTIONS] = to_pieces(og_ref).astype(BF16)

    @pl.when(last)
    def _():
        place_first[...] = place_matrix(own_info, True)

    pl.semaphore_wait(barrier, EXPERTS - 1 + SECTIONS - 1)

    def begin():
        scatter(place_first, h_all[0], send_first, f_recv, f_sem, sent_first, 0)

    @pl.when(jnp.logical_and(first, c == 0))
    def _():
        begin()

    @pl.when(last)
    def _():
        scatter(place_first, g_all[SECTIONS], send_first, b_recv, b_sem, sent_first, SECTIONS - 1)

    for k in range(1, SECTIONS):
        pl.semaphore_signal(planes_sem, inc=1, device_id=(lax.rem(s + k, SECTIONS), e), device_id_type=MESH)

    @pl.when(at_home)
    def _():
        notes[s] = note_own[...]

    @pl.when(jnp.logical_not(at_home))
    def _():
        remote(note_own, notes.at[s], sent_note, note_sem, home_plane(z, x), e)

    def dequant(code, steps, out, col, fan_in, groups):
        def one(g, carry):
            rows = pl.ds(pl.multiple_of(g * GROUP, GROUP), GROUP)
            scale = (steps[g] if len(steps.shape) == 3 else steps[pl.ds(g, 1), :]) * fan_in ** (-0.5)
            width = code.shape[1]
            out[rows, col : col + width] = ((code[rows, :].astype(F32) - 1.5) * scale).astype(BF16)
            return carry
        lax.fori_loop(0, groups, one, 0)

    loads[5].wait()
    loads[6].wait()
    dequant(gcode, gs_ref, w_gu, 0, WIDTH, WIDTH // GROUP)
    loads[7].wait()
    loads[8].wait()
    dequant(ucode, us_ref, w_gu, HIDDEN, WIDTH, WIDTH // GROUP)
    loads[9].wait()
    loads[10].wait()
    dequant(dcode, ds_ref, w_d, 0, HIDDEN, HIDDEN // GROUP)

    @pl.when(jnp.logical_and(first, c == 1))
    def _():
        begin()

    def info_of(layer):
        return notes[layer, 0:TOKENS, 0:128]

    pl.semaphore_wait(planes_sem, SECTIONS - 1)

    @pl.when(at_home)
    def _():
        wait_all(notes.at[pl.ds(0, SECTIONS - 1)], note_sem)
        take_w[0] = take_matrix(info_of(0), True)
        place_f[0] = place_matrix(info_of(1), False)

    def spread_out(recv, ch):
        flat = recv[ch].reshape(SOURCES * TILE, LANES).astype(F32)
        for half in range(2):
            wide[half] = flat[:, half * 128 : (half + 1) * 128]
        return [
            jnp.concatenate([wide[half, pl.ds(p, ROWS, stride=PIECES), :] for half in range(2)], axis=1)
            for p in range(PIECES)
        ]

    def collect(p, part):
        for half in range(2):
            wide[half, pl.ds(p, ROWS, stride=PIECES), :] = part[:, half * 128 : (half + 1) * 128]

    def rows_of(ch):
        return pl.ds(pl.multiple_of(ch * ROWS, ROWS), ROWS)

    def gates(ch):
        wait_all(f_recv.at[ch], f_sem.at[ch])
        parts = spread_out(f_recv, ch)
        square = functools.reduce(lambda a, b: a + b, [jnp.sum(q * q, axis=1, keepdims=True) for q in parts])
        inv = lax.rsqrt(square * (1.0 / WIDTH) + 1e-06)
        rows = rows_of(ch)
        for p in range(PIECES):
            lanes = slice(p * LANES, (p + 1) * LANES)
            x_rows[rows, lanes] = (parts[p] * inv * gain_ref[0:1, lanes]).astype(BF16)
        pre[rows, :] = dot(x_rows[rows, :], w_gu[...])
        gate, up = pre[rows, :HIDDEN], pre[rows, HIDDEN:]
        act[rows, :] = (gate * jax.nn.sigmoid(gate) * up).astype(BF16)

    def down(ch):
        rows = rows_of(ch)
        for p in range(PIECES):
            collect(p, dot(act[rows, :], w_d[:, p * LANES : (p + 1) * LANES]))
        give_back(ch, r_send, r_recv, r_sem, sent_r, False)

    def backward(ch):
        wait_all(b_recv.at[ch], b_sem.at[ch])
        parts = spread_out(b_recv, ch)
        rows = rows_of(ch)
        for p in range(PIECES):
            cot[rows, p * LANES : (p + 1) * LANES] = parts[p].astype(BF16)
        act_cot = dot(cot[rows, :], w_d[...], NT)
        gate, up = pre[rows, :HIDDEN], pre[rows, HIDDEN:]
        sig = jax.nn.sigmoid(gate)
        gu_cot[rows, :HIDDEN] = (act_cot * up * sig * (1.0 + gate * (1.0 - sig))).astype(BF16)
        gu_cot[rows, HIDDEN:] = (act_cot * gate * sig).astype(BF16)
        for p in range(PIECES):
            collect(p, dot(gu_cot[rows, :], w_gu[p * LANES : (p + 1) * LANES, :], NT))
        give_back(ch, q_send, q_recv, q_sem, sent_q, first)

    def home_forward(layer):
        wait_all(r_recv, r_sem)
        mixed = dot(take_w[layer], r_recv[...].reshape(EXPERTS * TILE, LANES))
        h_all[layer + 1] = (h_all[layer].astype(F32) + mixed).astype(BF16)

    def hand_output(layer):
        send_or_copy(h_all.at[layer + 1], lo_buf, sent_lo, lo_sem, layer, e, s == layer)

    def norm_back(matrix, hidden, gain8, above):
        wait_all(q_recv, q_sem)
        normed_cot = dot(matrix, q_recv[...].reshape(EXPERTS * TILE, LANES))
        hidden = hidden.astype(F32)
        inv = lax.rsqrt(token_sum(hidden * hidden) * (1.0 / WIDTH) + 1e-06)
        gain = jnp.broadcast_to(gain8.reshape(1, PIECES, LANES), (TOKENS, PIECES, LANES))
        scaled = gain.reshape(TOKENS * PIECES, LANES) * normed_cot
        mean = token_sum(scaled * hidden) * (1.0 / WIDTH)
        total = above.astype(F32) + inv * scaled - hidden * (inv * inv * inv) * mean
        return total.astype(BF16)

    def home_backward(layer):
        gain8 = notes[layer, TOKENS : TOKENS + PIECES, :]
        g_all[layer] = norm_back(take_1[layer - 1], h_all[layer], gain8, g_all[layer + 1])
        k = SECTIONS - 2 + layer
        scatter(place_b.at[layer - 1], g_all[layer], send_home.at[k], b_recv, b_sem, sent_home.at[k], layer - 1)
        send_or_copy(g_all.at[layer], ig_buf, sent_ig, ig_sem, layer, e, s == layer)

        @pl.when(layer == 1)
        def _():
            send_or_copy(g_all.at[layer], g1_buf, sent_g1, g1_sem, 0, e, s == 0)

        @pl.when(layer > 1)
        def _():
            prepare_back(layer - 1)

    def prepare_back(layer):
        take_1[layer - 1] = take_matrix(info_of(layer), False)
        place_b[layer - 1] = place_matrix(info_of(layer - 1), True)

    def step_grads():
        def gate_up(i, carry):
            rows = pl.ds(pl.multiple_of(i * 256, 256), 256)
            for code, out, col in ((gcode, gg_ref, 0), (ucode, ug_ref, HIDDEN)):
                grad = dot(x_rows[:, rows], gu_cot[:, col : col + HIDDEN], TN)
                grad = grad * (code[rows, :].astype(F32) - 1.5)
                summed = jnp.sum(grad.reshape(256 // GROUP, GROUP, HIDDEN), axis=1) * WIDTH ** (-0.5)
                for g in range(256 // GROUP):
                    out[pl.ds(i * (256 // GROUP) + g, 1), :] = summed[g : g + 1, :]
            return carry

        lax.fori_loop(0, WIDTH // 256, gate_up, 0)

        def down_part(i, carry):
            rows = pl.ds(pl.multiple_of(i * 256, 256), 256)
            for col in range(0, WIDTH, 1024):
                grad = dot(act[:, rows], cot[:, col : col + 1024], TN)
                grad = grad * (dcode[rows, col : col + 1024].astype(F32) - 1.5)
                summed = jnp.sum(grad.reshape(256 // GROUP, GROUP, 1024), axis=1) * HIDDEN ** (-0.5)
                for g in range(256 // GROUP):
                    dg_ref[i * (256 // GROUP) + g, :, col : col + 1024] = summed[g : g + 1, :]
            return carry

        lax.fori_loop(0, HIDDEN // 256, down_part, 0)

    def forward_layer(layer, carry):
        @pl.when(s == layer)
        def _():
            def expert(ch, carry):
                gates(ch)
                down(ch)
                return carry

            lax.fori_loop(0, CHAINS, expert, 0)

        @pl.when(at_home)
        def _():
            home_forward(layer)
            scatter(
                place_f.at[layer], h_all[layer + 1], send_home.at[layer], f_recv, f_sem, sent_home.at[layer], layer + 1
            )
            hand_output(layer)
            take_w[layer + 1] = take_matrix(info_of(layer + 1), True)

            @pl.when(layer < SECTIONS - 2)
            def _():
                place_f[layer + 1] = place_matrix(info_of(layer + 2), False)

            @pl.when(layer == SECTIONS - 2)
            def _():
                prepare_back(SECTIONS - 1)

        return carry

    lax.fori_loop(0, SECTIONS - 1, forward_layer, 0)

    @pl.when(first)
    def _():
        take_last[...] = take_matrix(own_info, False)

    def backward_layer(t, carry):
        layer = SECTIONS - 1 - t

        @pl.when(s == layer)
        def _():
            def expert(ch, carry):
                @pl.when(last)
                def _():
                    gates(ch)

                backward(ch)
                return carry

            lax.fori_loop(0, CHAINS, expert, 0)

        @pl.when(jnp.logical_and(at_home, layer > 0))
        def _():
            home_backward(layer)

        @pl.when(jnp.logical_and(last, layer == SECTIONS - 1))
        def _():
            def give(ch, carry):
                down(ch)
                return carry

            lax.fori_loop(0, CHAINS, give, 0)

        @pl.when(s == layer)
        def _():
            step_grads()

        @pl.when(jnp.logical_and(at_home, t == 1))
        def _():
            home_forward(SECTIONS - 1)
            hand_output(SECTIONS - 1)

        return carry

    lax.fori_loop(0, SECTIONS, backward_layer, 0)

    wait_all(lo_buf, lo_sem)
    from_pieces(lo_buf[...].astype(F32), lo_ref)

    @pl.when(first)
    def _():
        wait_all(g1_buf, g1_sem)
        gain8 = note_own[TOKENS : TOKENS + PIECES, :]
        g_final[...] = norm_back(take_last[...], h_all[0], gain8, g1_buf[...])
        from_pieces(g_final[...].astype(F32), ig_ref)

    @pl.when(s > 0)
    def _():
        wait_all(ig_buf, ig_sem)
        from_pieces(ig_buf[...].astype(F32), ig_ref)

    def wait_messages(sem, some, own):
        @pl.when(own)
        def _():
            wait_all(some.at[pl.ds(0, EXPERTS - 1)], sem)

        @pl.when(jnp.logical_not(own))
        def _():
            wait_all(some, sem)

    @pl.when(jnp.logical_or(first, last))
    def _():
        wait_all(send_first.at[pl.ds(0, EXPERTS - 1)], sent_first)

    wait_messages(sent_r, send_first, at_home)
    wait_messages(sent_q, send_first, jnp.logical_or(at_home, first))

    @pl.when(jnp.logical_not(at_home))
    def _():
        wait_all(note_own, sent_note)

    @pl.when(at_home)
    def _():
        for layer in range(SECTIONS - 1):
            wait_messages(sent_home.at[layer], send_first, s == layer + 1)
            wait_messages(sent_home.at[SECTIONS - 1 + layer], send_first, s == layer)
        wait_all(h_all.at[pl.ds(0, SECTIONS - 1)], sent_lo)

        @pl.when(first)
        def _():
            wait_all(g_all.at[pl.ds(0, SECTIONS - 1)], sent_ig)

        @pl.when(s > 0)
        def _():
            wait_all(g_all.at[pl.ds(0, SECTIONS - 2)], sent_ig)
            wait_all(g1_buf, sent_g1)


def give_out(*refs):
    count = len(refs) // 3
    taken, given, held, sems = refs[:count], refs[count : 2 * count], refs[2 * count : 3 * count], refs[-1]
    loads = [pltpu.make_async_copy(taken[k], held[k], sems.at[0, k]) for k in range(count)]
    stores = [pltpu.make_async_copy(held[k], given[k], sems.at[1, k]) for k in range(count)]
    for load in loads:
        load.start()
    for load, store in zip(loads, stores):
        load.wait()
        store.start()
    for store in stores:
        store.wait()


def body(inputs, norm_gain, expert_ids, route_weights, gate_codes, up_codes, down_codes, gate_steps, up_steps, down_steps, out_grad):
    vmem = pl.BlockSpec(memory_space=pltpu.VMEM)
    hbm = pl.BlockSpec(memory_space=pl.ANY)
    message = (TILE, LANES)
    pieces = (TOKENS * PIECES, LANES)
    slots = EXPERTS * TILE
    both = CHAINS * ROWS
    steps = SECTIONS - 1
    tokens = (TOKENS, WIDTH)
    gate_shape, down_shape = (WIDTH, HIDDEN), (HIDDEN, WIDTH)
    gate_steps_shape, down_steps_shape = (WIDTH // GROUP, HIDDEN), (HIDDEN // GROUP, WIDTH)
    place, take = (slots, TOKENS * PIECES), (TOKENS * PIECES, slots)
    dma = pltpu.SemaphoreType.DMA
    scratch = [
        pltpu.VMEM(tokens, BF16),
        pltpu.VMEM(tokens, BF16),
        pltpu.VMEM((1, WIDTH), F32),
        pltpu.VMEM((TOP, TOKENS), jnp.int32),
        pltpu.VMEM((TOP, TOKENS), F32),
        pltpu.VMEM(gate_steps_shape, F32),
        pltpu.VMEM(gate_steps_shape, F32),
        pltpu.VMEM((HIDDEN // GROUP, 1, WIDTH), F32),
        pltpu.VMEM(gate_shape, BF16),
        pltpu.VMEM(gate_shape, BF16),
        pltpu.VMEM(down_shape, BF16),
        pltpu.VMEM((WIDTH, 2 * HIDDEN), BF16),
        pltpu.VMEM(down_shape, BF16),
        pltpu.VMEM((CHAINS, SOURCES) + message, BF16),
        pltpu.VMEM((EXPERTS,) + message, BF16),
        pltpu.VMEM((CHAINS, SOURCES) + message, BF16),
        pltpu.VMEM((EXPERTS,) + message, BF16),
        pltpu.VMEM((EXPERTS,) + message, BF16),
        pltpu.VMEM((2 * steps, EXPERTS) + message, BF16),
        pltpu.VMEM((CHAINS, SOURCES) + message, BF16),
        pltpu.VMEM((CHAINS, SOURCES) + message, BF16),
        pltpu.VMEM(place, BF16),
        pltpu.VMEM((steps,) + place, BF16),
        pltpu.VMEM((steps,) + place, BF16),
        pltpu.VMEM((SECTIONS,) + take, BF16),
        pltpu.VMEM((steps,) + take, BF16),
        pltpu.VMEM(take, BF16),
        pltpu.VMEM((SECTIONS + 1,) + pieces, BF16),
        pltpu.VMEM((SECTIONS + 1,) + pieces, BF16),
        pltpu.VMEM(pieces, BF16),
        pltpu.VMEM(pieces, BF16),
        pltpu.VMEM(pieces, BF16),
        pltpu.VMEM(pieces, BF16),
        pltpu.VMEM((TOKENS + PIECES, LANES), F32),
        pltpu.VMEM((SECTIONS, TOKENS + PIECES, LANES), F32),
        pltpu.VMEM((2, SOURCES * TILE, 128), F32),
        pltpu.VMEM((2, TOKENS * PIECES, 128), F32),
        pltpu.VMEM((both, WIDTH), BF16),
        pltpu.VMEM((both, 2 * HIDDEN), F32),
        pltpu.VMEM((both, HIDDEN), BF16),
        pltpu.VMEM((both, WIDTH), BF16),
        pltpu.VMEM((both, 2 * HIDDEN), BF16),
        dma((11,)),
        dma((CHAINS,)),
        dma,
        dma((CHAINS,)),
        dma,
        dma,
        dma,
        dma,
        dma,
        dma,
        dma((2 * steps,)),
        dma,
        dma,
        dma,
        dma,
        dma,
        dma,
        pltpu.SemaphoreType.REGULAR,
    ]
    outs = pl.pallas_call(
        kernel,
        out_shape=(
            jax.ShapeDtypeStruct(tokens, BF16),
            jax.ShapeDtypeStruct(tokens, BF16),
            jax.ShapeDtypeStruct(gate_steps_shape, F32),
            jax.ShapeDtypeStruct(gate_steps_shape, F32),
            jax.ShapeDtypeStruct((HIDDEN // GROUP, 1, WIDTH), F32),
        ),
        in_specs=[hbm] * 11,
        out_specs=[vmem] * 5,
        scratch_shapes=scratch,
        compiler_params=pltpu.CompilerParams(
            collective_id=0, has_side_effects=True, vmem_limit_bytes=58 * 1024 * 1024
        ),
    )(
        inputs[0], norm_gain, jnp.transpose(expert_ids[0, 0]), jnp.transpose(route_weights[0, 0]),
        gate_codes[0, 0], up_codes[0, 0], down_codes[0, 0],
        gate_steps[0, 0], up_steps[0, 0], jnp.transpose(down_steps[0], (1, 0, 2)), out_grad[0],
    )
    layer_out, input_grad, gate_grad, up_grad, down_grad = pl.pallas_call(
        give_out,
        out_shape=tuple(jax.ShapeDtypeStruct(out.shape, out.dtype) for out in outs),
        in_specs=[hbm] * len(outs),
        out_specs=[hbm] * len(outs),
        scratch_shapes=[pltpu.VMEM(out.shape, out.dtype) for out in outs] + [dma((2, len(outs)))],
    )(*outs)
    return (layer_out[None, None], input_grad[None, None], gate_grad[None, None], up_grad[None, None], jnp.transpose(down_grad, (1, 0, 2))[None])


def solution(mesh):
    in_specs = (
        P(None, "expert", None),
        P("section", None),
        P("section", None, "expert", None),
        P("section", None, "expert", None),
        P("section", "expert", None, None),
        P("section", "expert", None, None),
        P("section", "expert", None, None),
        P("section", "expert", None, None),
        P("section", "expert", None, None),
        P("section", "expert", None, None),
        P(None, "expert", None),
    )
    out_specs = (
        P("section", None, "expert", None),
        P("section", None, "expert", None),
        P("section", "expert", None, None),
        P("section", "expert", None, None),
        P("section", "expert", None, None),
    )
    return jax.shard_map(body, mesh=mesh, in_specs=in_specs, out_specs=out_specs, check_vma=False)
```

time: 240 us -> 185 us (0.77)
  Pallas kernels: 227 us -> 184 us
  local copies, waits for them, and re-layouts: 11.9 us -> 0 us
    pallas_call x1 -> x2, Pallas kernels: 227 us -> 184 us  [the longest x1 182 us: body(): pl.pallas_call(kernel, out_shape=(jax.ShapeDtypeStruct(tokens, BF16), jax...]
    unnamed x18 -> x0, local copies, waits for them, and re-layouts: 10.4 us -> none
where the time goes in v1:
time: 185 us
  Pallas kernels  184 us (99%)
    pallas_call x1, Pallas kernels, body(): pl.pallas_call(kernel, out_shape=(jax.ShapeDtypeStruct(tokens, BF16), jax...  182 us

profile of v1, /device:TPU:1, one launch (start us, length us, event | category | flops | bytes accessed | tf_op | source)
XLA Modules:
  0.0 185.0 jit_solution(14879672557135271522)
XLA Ops:
  0.6 182.4 %shard_map.146 = (bf16[32,2048]{1,0:T(8,128)(2,1)}, bf16[32,2048]{1,0:T(8,128)(2,1)}, f32[32,768]{1,0:T(8,128)}, f32[32,768]{1,0:T(8,128)}, f32[12,1,2048]{2,1,0:T(1,128)}) custom-call(bf16[32,2048]{1,0:T(8,128)(2,1)} %bitcast.24, f32[1,2048]{1,0:T(1,128)} %gain_hbm.1, s32[2,32]{1,0:T(2,128)} %bitcast.29, f32[2,32]{1,0:T(2,128)} %bitcast.30, ...), custom_call_target="tpu_custom_call" | custom-call | tf_op jit(solution)/shard_map/pallas_call | solution.py:642
  183.0 1.8 shard_map.147

commit v2 on v1

--- a/solution.py
+++ b/solution.py
@@ -88,12 +88,12 @@
     lo_ref, ig_ref, gg_ref, ug_ref, dg_ref,
     x_ref, og_ref, gain_ref, ids_ref, wts_ref, gs_ref, us_ref, ds_ref,
     gcode, ucode, dcode, w_gu, w_d,
-    f_recv, r_recv, b_recv, q_recv, send_first, send_home, r_send, q_send,
+    f_recv, r_recv, b_recv, q_recv, send_first, send_home, r_send, q_send, relay_send, relay_recv,
     place_first, place_f, place_b, take_w, take_1, take_last,
     h_all, g_all, g_final, lo_buf, ig_buf, g1_buf, note_own, notes,
     wide, home, x_rows, pre, act, cot, gu_cot,
     load_sem, f_sem, r_sem, b_sem, q_sem, note_sem, lo_sem, ig_sem, g1_sem,
-    sent_first, sent_home, sent_r, sent_q, sent_note, sent_lo, sent_ig, sent_g1, planes_sem,
+    sent_first, sent_home, sent_r, sent_q, sent_note, sent_lo, sent_ig, sent_g1, planes_sem, relay_sem, sent_relay, sent_on,
 ):
     s = lax.axis_index("section")
     e = lax.axis_index("expert")
@@ -193,7 +193,7 @@
         send(NZ - 1, 0, 1)
         send_or_copy(buffer.at[e], recv.at[chain, order], ssem, rsem.at[chain], section, e, section == s)
 
-    def give_back(ch, buffer, recv, rsem, ssem, in_plane):
+    def give_back(ch, buffer, recv, rsem, ssem, in_plane, lap):
         def unpack(j):
             zz = far_z(j)
             block = pl.ds(pl.multiple_of(zz * NX * TILE, 64), NX * TILE)
@@ -223,11 +223,63 @@
             send(j, 0)
             return carry
 
-        lax.fori_loop(0, NZ, farthest, 0)
-        lax.fori_loop(0, NZ, middle, 0)
-        lax.fori_loop(0, NZ - 1, line, 0)
-        src, section, target = place_of(NZ - 1, 0)
-        send_or_copy(src, recv.at[e], ssem, rsem, section, target, jnp.logical_and(section == s, ch == c))
+        def rest():
+            src, section, target = place_of(NZ - 1, 0)
+            send_or_copy(src, recv.at[e], ssem, rsem, section, target, jnp.logical_and(section == s, ch == c))
+
+        if lap is None:
+            lax.fori_loop(0, NZ, farthest, 0)
+            lax.fori_loop(0, NZ, middle, 0)
+            lax.fori_loop(0, NZ - 1, line, 0)
+            rest()
+            return
+
+        half = lap // (SECTIONS - 1)
+        def gather(j, carry):
+            unpack(j)
+            zz = far_z(j)
+            for k in range(SECTIONS - 1):
+                xx = lax.rem(s + 1 + k + 2 * NZ - zz, NX)
+                relay_send[ch, half, k, j - 5] = buffer[ch, zz * NX + xx]
+            return carry
+
+        lax.fori_loop(5, 7, gather, 0)
+        for k in (1, 0, 2):
+            remote(
+                relay_send.at[ch, half, k], relay_recv.at[lap, ch], sent_relay, relay_sem.at[lap, ch],
+                lax.rem(s + 1 + k, SECTIONS), e,
+            )
+        lax.fori_loop(0, 5, farthest, 0)
+        lax.fori_loop(0, 5, middle, 0)
+        lax.fori_loop(0, 5, line, 0)
+
+        def near(j, carry):
+            zz = far_z(j)
+            xx = lax.rem(s + 2 * NZ - zz, NX)
+            remote(buffer.at[ch, zz * NX + xx], recv.at[e], ssem, rsem, s, index_of(zz, xx, ch))
+            return carry
+
+        lax.fori_loop(5, 7, near, 0)
+        unpack(NZ - 1)
+        send(NZ - 1, 2)
+        send(NZ - 1, 1)
+        send(NZ - 1, 3)
+        rest()
+
+    def relay(lap, recv, rsem):
+        def one(ch, carry):
+            wait_all(relay_recv.at[lap, ch], relay_sem.at[lap, ch])
+
+            def on(j, carry):
+                zz = far_z(j)
+                xx = lax.rem(s + 2 * NZ - zz, NX)
+                remote(relay_recv.at[lap, ch, j - 5], recv.at[e], sent_on, rsem, s, index_of(zz, xx, ch))
+                return carry
+
+            lax.fori_loop(5, 7, on, 0)
+            return carry
+
+        lax.fori_loop(0, CHAINS, one, 0)
 
     loads[0].wait()
     loads[1].wait()
@@ -339,11 +391,11 @@
         gate, up = pre[rows, :HIDDEN], pre[rows, HIDDEN:]
         act[rows, :] = (gate * jax.nn.sigmoid(gate) * up).astype(BF16)
 
-    def down(ch):
+    def down(ch, lap):
         rows = rows_of(ch)
         for p in range(PIECES):
             collect(p, dot(act[rows, :], w_d[:, p * LANES : (p + 1) * LANES]))
-        give_back(ch, r_send, r_recv, r_sem, sent_r, False)
+        give_back(ch, r_send, r_recv, r_sem, sent_r, False, lap)
 
     def backward(ch):
         wait_all(b_recv.at[ch], b_sem.at[ch])
@@ -358,7 +410,14 @@
         gu_cot[rows, HIDDEN:] = (act_cot * gate * sig).astype(BF16)
         for p in range(PIECES):
             collect(p, dot(gu_cot[rows, :], w_gu[p * LANES : (p + 1) * LANES, :], NT))
-        give_back(ch, q_send, q_recv, q_sem, sent_q, first)
+
+        @pl.when(first)
+        def _():
+            give_back(ch, q_send, q_recv, q_sem, sent_q, True, None)
+
+        @pl.when(s > 0)
+        def _():
+            give_back(ch, q_send, q_recv, q_sem, sent_q, False, SECTIONS - 2 + s)
 
     def home_forward(layer):
         wait_all(r_recv, r_sem)
@@ -428,10 +487,14 @@
         def _():
             def expert(ch, carry):
                 gates(ch)
-                down(ch)
+                down(ch, layer)
                 return carry
 
             lax.fori_loop(0, CHAINS, expert, 0)
+
+        @pl.when(s != layer)
+        def _():
+            relay(layer, r_recv, r_sem)
 
         @pl.when(at_home)
         def _():
@@ -473,6 +536,10 @@
 
             lax.fori_loop(0, CHAINS, expert, 0)
 
+        @pl.when(jnp.logical_and(s != layer, layer > 0))
+        def _():
+            relay(SECTIONS - 2 + layer, q_recv, q_sem)
+
         @pl.when(jnp.logical_and(at_home, layer > 0))
         def _():
             home_backward(layer)
@@ -480,7 +547,7 @@
         @pl.when(jnp.logical_and(last, layer == SECTIONS - 1))
         def _():
             def give(ch, carry):
-                down(ch)
+                down(ch, None)
                 return carry
 
             lax.fori_loop(0, CHAINS, give, 0)
@@ -526,8 +593,20 @@
     def _():
         wait_all(send_first.at[pl.ds(0, EXPERTS - 1)], sent_first)
 
-    wait_messages(sent_r, send_first, at_home)
-    wait_messages(sent_q, send_first, jnp.logical_or(at_home, first))
+    own = jnp.where(at_home, 1, 0)
+
+    def wait_count(sem, count):
+        def one(k, carry):
+            wait_all(send_first.at[0], sem)
+            return carry
+
+        lax.fori_loop(0, count, one, 0)
+
+    direct, ways = 26 * CHAINS, (SECTIONS - 1) * CHAINS
+    wait_count(sent_r, jnp.where(last, EXPERTS, direct) - own)
+    wait_count(sent_q, jnp.where(first, EXPERTS - 1, direct - own))
+    wait_count(sent_relay, jnp.where(jnp.logical_or(first, last), 1, 2) * (2 * ways))
+    wait_count(sent_on, 2 * CHAINS * jnp.where(first, 2 + 3, jnp.where(last, 3 + 2, 2 + 2)))
 
     @pl.when(jnp.logical_not(at_home))
     def _():
@@ -599,6 +678,8 @@
         pltpu.VMEM((2 * steps, EXPERTS) + message, BF16),
         pltpu.VMEM((CHAINS, SOURCES) + message, BF16),
         pltpu.VMEM((CHAINS, SOURCES) + message, BF16),
+        pltpu.VMEM((CHAINS, 2, steps, 2) + message, BF16),
+        pltpu.VMEM((2 * steps, CHAINS, 2) + message, BF16),
         pltpu.VMEM(place, BF16),
         pltpu.VMEM((steps,) + place, BF16),
         pltpu.VMEM((steps,) + place, BF16),
@@ -638,6 +719,9 @@
         dma,
         dma,
         pltpu.SemaphoreType.REGULAR,
+        dma((2 * steps, CHAINS)),
+        dma,
+        dma,
     ]
     outs = pl.pallas_call(
         kernel,

time: 185 us -> 180 us (0.973)
  Pallas kernels: 184 us -> 179 us
    pallas_call x1, Pallas kernels: 182 us -> 177 us  [body(): pl.pallas_call(kernel, out_shape=(jax.ShapeDtypeStruct(tokens, BF16), jax...]
where the time goes in v2:
time: 180 us; the launch traced here: 179 us
  Pallas kernels  179 us (99%)
    pallas_call x1, Pallas kernels, body(): pl.pallas_call(kernel, out_shape=(jax.ShapeDtypeStruct(tokens, BF16), jax...  177 us

profile of v2, /device:TPU:1, one launch (start us, length us, event | category | flops | bytes accessed | tf_op | source)
XLA Modules:
  0.0 179.4 jit_solution(3954396407473484724)
XLA Ops:
  0.6 176.8 %shard_map.146 = (bf16[32,2048]{1,0:T(8,128)(2,1)}, bf16[32,2048]{1,0:T(8,128)(2,1)}, f32[32,768]{1,0:T(8,128)}, f32[32,768]{1,0:T(8,128)}, f32[12,1,2048]{2,1,0:T(1,128)}) custom-call(bf16[32,2048]{1,0:T(8,128)(2,1)} %bitcast.24, f32[1,2048]{1,0:T(1,128)} %gain_hbm.1, s32[2,32]{1,0:T(2,128)} %bitcast.29, f32[2,32]{1,0:T(2,128)} %bitcast.30, ...), custom_call_target="tpu_custom_call" | custom-call | tf_op jit(solution)/shard_map/pallas_call | solution.py:726
  177.4 1.8 %shard_map.147 = (bf16[32,2048]{1,0:T(8,128)(2,1)}, bf16[32,2048]{1,0:T(8,128)(2,1)}, f32[32,768]{1,0:T(8,128)}, f32[32,768]{1,0:T(8,128)}, f32[12,1,2048]{2,1,0:T(1,128)}) custom-call(bf16[32,2048]{1,0:T(8,128)(2,1)} %get-tuple-element.15.refs_0_, bf16[32,2048]{1,0:T(8,128)(2,1)} %get-tuple-element.16.refs_1_, f32[32,768]{1,0:T(8,128)} %get-tuple-element.17.refs_2_, ...), custom_call_target="tpu_custom_call" | custom-call | tf_op jit(solution)/shard_map/pallas_call | solution.py:746

commit v3 on v2

--- a/solution.py
+++ b/solution.py
@@ -428,10 +428,10 @@
         send_or_copy(h_all.at[layer + 1], lo_buf, sent_lo, lo_sem, layer, e, s == layer)
 
     def norm_back(matrix, hidden, gain8, above):
+        hidden = hidden.astype(F32)
+        inv = lax.rsqrt(token_sum(hidden * hidden) * (1.0 / WIDTH) + 1e-06)
         wait_all(q_recv, q_sem)
         normed_cot = dot(matrix, q_recv[...].reshape(EXPERTS * TILE, LANES))
-        hidden = hidden.astype(F32)
-        inv = lax.rsqrt(token_sum(hidden * hidden) * (1.0 / WIDTH) + 1e-06)
         gain = jnp.broadcast_to(gain8.reshape(1, PIECES, LANES), (TOKENS, PIECES, LANES))
         scaled = gain.reshape(TOKENS * PIECES, LANES) * normed_cot
         mean = token_sum(scaled * hidden) * (1.0 / WIDTH)

time: 180 us -> 180 us (level)
  no operation moved by 1% of the time
where the time goes in v3:
time: 180 us
  Pallas kernels  179 us (99%)
    pallas_call x1, Pallas kernels, body(): pl.pallas_call(kernel, out_shape=(jax.ShapeDtypeStruct(tokens, BF16), jax...  177 us

profile of v3, /device:TPU:1, one launch (start us, length us, event | category | flops | bytes accessed | tf_op | source)
XLA Modules:
  0.0 180.1 jit_solution(16225510270631805353)
XLA Ops:
  0.6 177.5 %shard_map.146 = (bf16[32,2048]{1,0:T(8,128)(2,1)}, bf16[32,2048]{1,0:T(8,128)(2,1)}, f32[32,768]{1,0:T(8,128)}, f32[32,768]{1,0:T(8,128)}, f32[12,1,2048]{2,1,0:T(1,128)}) custom-call(bf16[32,2048]{1,0:T(8,128)(2,1)} %bitcast.24, f32[1,2048]{1,0:T(1,128)} %gain_hbm.1, s32[2,32]{1,0:T(2,128)} %bitcast.29, f32[2,32]{1,0:T(2,128)} %bitcast.30, ...), custom_call_target="tpu_custom_call" | custom-call | tf_op jit(solution)/shard_map/pallas_call | solution.py:726
  178.1 1.8 %shard_map.147 = (bf16[32,2048]{1,0:T(8,128)(2,1)}, bf16[32,2048]{1,0:T(8,128)(2,1)}, f32[32,768]{1,0:T(8,128)}, f32[32,768]{1,0:T(8,128)}, f32[12,1,2048]{2,1,0:T(1,128)}) custom-call(bf16[32,2048]{1,0:T(8,128)(2,1)} %get-tuple-element.15.refs_0_, bf16[32,2048]{1,0:T(8,128)(2,1)} %get-tuple-element.16.refs_1_, f32[32,768]{1,0:T(8,128)} %get-tuple-element.17.refs_2_, ...), custom_call_target="tpu_custom_call" | custom-call | tf_op jit(solution)/shard_map/pallas_call | solution.py:746
